TPU v7x, 32 devices: a whole 2x2x4 slice. The times are simulated.
32 devices in a mesh: wide: 8 (over z, y), narrow: 4 (over x, core).
Axes of the slice: x: 2, y: 2, z: 4, core: 2. Of those that a mesh axis runs over, the one named last changes fastest.
Arguments:
- buoy_coef: bfloat16 [4, 512, 1024], P(None, 'narrow', 'wide'), may hold values from -300 to 300, as said below
- velocity: bfloat16 [3, 4, 768, 1536], P(None, 'narrow', 'wide'), may hold values from -6 to 6
- buoy_dy: bfloat16 [4, 768, 1536], P('narrow', 'wide'), may hold values from -6 to 6
Outputs:
- advect: bfloat16 [4, 512, 1024], P(None, 'narrow', 'wide')
- buoy_grid: bfloat16 [4, 768, 1536], P('narrow', 'wide')
Inputs may be any that keep to these rules, and one draw needn't show every extreme that they name: `buoy_coef`: spectral coefficients of the buoyancy.
All inputs are finite; a program needn't handle non-finite values.
Results may differ from a plain program's by a relative error of at most 0.0087.
Values may be sent and summed in bfloat16 or wider, within the bound.
A program may use at most 64 MiB of HBM per device.

v0:
```python
import functools
import math

import jax
import jax.numpy as jnp
import ml_dtypes
import numpy as np
from jax import lax
from jax.experimental import pallas as pl
from jax.experimental.pallas import tpu as pltpu
from jax.sharding import PartitionSpec as P

MESH = pl.DeviceIdType.MESH
F32 = jnp.float32
BF16 = jnp.bfloat16
LANES = 128


def x_table(gx_size, kx_size):
    points = np.arange(gx_size, dtype=np.int32)[:, None]
    column_id = np.arange(kx_size, dtype=np.int32)[None, :]
    harmonic = column_id // 2
    angles = (harmonic * points % gx_size).astype(np.float32) * np.float32(2.0 * math.pi / gx_size)
    weights = np.where(
        harmonic == 0, math.sqrt(1.0 / gx_size), math.sqrt(2.0 / gx_size)
    ).astype(np.float32)
    raw = np.where(column_id % 2 == 0, np.cos(angles), np.sin(angles))
    return (raw * weights).astype(ml_dtypes.bfloat16)


def z_tables(gz_size, kz_size):
    nodes = np.arange(gz_size, dtype=np.int32)[:, None]
    degree = np.arange(kz_size, dtype=np.int32)[None, :]
    step = np.float32(math.pi / (2.0 * gz_size))
    angles = (degree * (2 * nodes + 1) % (4 * gz_size)).astype(np.float32) * step
    polar = (2 * nodes + 1).astype(np.float32) * step
    weights = np.where(
        degree == 0, math.sqrt(1.0 / gz_size), math.sqrt(2.0 / gz_size)
    ).astype(np.float32)
    values = weights * np.cos(angles)
    slopes = weights * np.float32(2.0 / gz_size) * degree.astype(np.float32)
    slopes = slopes * np.sin(angles) / np.sin(polar)
    return values.astype(ml_dtypes.bfloat16), slopes.astype(ml_dtypes.bfloat16)


def dot(left, right):
    return jnp.dot(left, right, preferred_element_type=F32)


def flip_bits(index, mask, size):
    total, bit = 0, 1
    while bit < size:
        digit = lax.rem(lax.div(index, bit), 2)
        total = total + bit * (1 - digit if mask & bit else digit)
        bit *= 2
    return total


def kernel(
    wide, narrow, rows, gx_size,
    coef, velocity, slope_y, zt_hbm, bt_hbm, b_hbm, vt_hbm,
    advect_out, grid_out,
    zt, bt, b, vt, speed, dy,
    recv_a, send_b, recv_b, acc, adv, buoy, send_e, recv_e, send_f,
    local_sem, a_send, a_recv, b_send, b_recv, e_send, e_recv, f_send, f_recv,
):
    pairs = wide // 2
    w = lax.axis_index("wide")
    m = lax.axis_index("narrow")
    mine = lax.div(w, 2)
    beside = 2 * mine + 1 - lax.rem(w, 2)
    narrow_peers = [lax.rem(m + r, narrow) for r in range(1, narrow)]
    pair_of = [flip_bits(mine, t, pairs) for t in range(pairs)]
    far_first = list(range(pairs - 1, 0, -1))

    own = pltpu.make_async_copy(coef.at[m], recv_a.at[m], local_sem.at[0])
    own.start()
    loads = [
        pltpu.make_async_copy(src, dst, local_sem.at[1 + i])
        for i, (src, dst) in enumerate(
            [(zt_hbm, zt), (bt_hbm, bt), (velocity, speed), (slope_y, dy), (b_hbm, b), (vt_hbm, vt)]
        )
    ]
    for load in loads:
        load.start()

    barrier = pltpu.get_barrier_semaphore()
    for peer in narrow_peers:
        pl.semaphore_signal(barrier, inc=1, device_id={"narrow": peer}, device_id_type=MESH)
    for t in range(1, wide):
        pl.semaphore_signal(
            barrier, inc=1, device_id={"wide": lax.rem(w + t, wide)}, device_id_type=MESH
        )
    pl.semaphore_wait(barrier, narrow + wide - 2)

    sends = []

    def push(src, dst, send_sem, recv_sem, target):
        copy = pltpu.make_async_remote_copy(
            src_ref=src, dst_ref=dst, send_sem=send_sem, recv_sem=recv_sem,
            device_id=target, device_id_type=MESH,
        )
        copy.start()
        sends.append(copy)

    def arrived(dst, recv_sem, send_sem, target):
        pltpu.make_async_remote_copy(
            src_ref=dst, dst_ref=dst, send_sem=send_sem, recv_sem=recv_sem,
            device_id=target, device_id_type=MESH,
        ).wait_recv()

    for peer in narrow_peers:
        push(coef.at[peer], recv_a.at[m], a_send.at[peer], a_recv.at[m], {"narrow": peer})
    own.wait()
    loads[0].wait()
    for peer in narrow_peers:
        arrived(recv_a.at[peer], a_recv.at[peer], a_send.at[peer], {"narrow": peer})

    plane = recv_a[...].reshape(-1, LANES)

    def send_points(d):
        send_b[d] = dot(zt[d], plane).astype(BF16)
        push(send_b.at[d], recv_b.at[w], b_send.at[d], b_recv.at[w], {"wide": d})

    for t in far_first:
        send_points(2 * pair_of[t])
        send_points(2 * pair_of[t] + 1)
    send_points(beside)
    recv_b[w] = dot(zt[w], plane).astype(BF16)

    lane = lax.broadcasted_iota(jnp.int32, (1, LANES), 1)
    even = lax.rem(lane, 2) == 0

    def slope_of(field, first):
        harmonic = (lax.div(lane, 2) + first).astype(F32)
        rate = harmonic * (2.0 * math.pi / gx_size)
        wide_field = field.astype(F32)
        after = pltpu.roll(wide_field, LANES - 1, 1)
        before = pltpu.roll(wide_field, 1, 1)
        return jnp.where(even, rate * after, -rate * before).astype(BF16)

    def stacked(pair):
        fields = []
        for s in (0, 1):
            block = recv_b[2 * pair + s]
            val, dz = block[:rows], block[rows:]
            dx = slope_of(val, (2 * pair + s) * (LANES // 2))
            fields.append(jnp.concatenate([val, dx, dz], axis=0))
        return jnp.concatenate(fields, axis=1)

    tile = 512
    cuts = [slice(c, c + tile) for c in range(0, gx_size, tile)]
    for t in range(pairs):
        pair = pair_of[t]
        if t == 0:
            arrived(recv_b.at[beside], b_recv.at[beside], b_send.at[beside], {"wide": beside})
            loads[1].wait()
        else:
            for d in (2 * pair, 2 * pair + 1):
                arrived(recv_b.at[d], b_recv.at[d], b_send.at[d], {"wide": d})
        fields = stacked(pair)
        if t == pairs - 1:
            loads[2].wait()
            loads[3].wait()
        for cut in cuts:
            part = dot(fields, bt[pair, :, cut])
            if t > 0:
                part = part + acc[:, cut]
            if t < pairs - 1:
                acc[:, cut] = part
            else:
                buoy[0, :, cut] = part[:rows].astype(BF16)
                total = speed[0, 0, :, cut].astype(F32) * part[rows : 2 * rows]
                total = total + speed[1, 0, :, cut].astype(F32) * dy[0, :, cut].astype(F32)
                total = total + speed[2, 0, :, cut].astype(F32) * part[2 * rows :]
                adv[:, cut] = (-total).astype(BF16)
    grid_copy = pltpu.make_async_copy(buoy, grid_out, local_sem.at[7])
    grid_copy.start()

    loads[4].wait()
    for t in far_first + [0]:
        pair = pair_of[t]
        half = dot(adv[...], b[pair]).astype(BF16)
        for s in (0, 1):
            send_e[2 * pair + s] = half[:, s * LANES : (s + 1) * LANES]
        for d in (2 * pair, 2 * pair + 1) if t else (beside,):
            push(send_e.at[d], recv_e.at[w], e_send.at[d], e_recv.at[w], {"wide": d})
    recv_e[w] = send_e[w]
    loads[5].wait()
    for t in range(pairs):
        for d in (2 * pair_of[t], 2 * pair_of[t] + 1) if t else (beside,):
            arrived(recv_e.at[d], e_recv.at[d], e_send.at[d], {"wide": d})

    points = recv_e[...].reshape(-1, LANES)
    for peer in narrow_peers:
        send_f[peer] = dot(vt[peer], points).astype(BF16)
        push(send_f.at[peer], advect_out.at[m], f_send.at[peer], f_recv.at[m], {"narrow": peer})
    advect_out[m] = dot(vt[m], points).astype(BF16)
    for peer in narrow_peers:
        arrived(advect_out.at[peer], f_recv.at[peer], f_send.at[peer], {"narrow": peer})
    grid_copy.wait()
    for copy in sends:
        copy.wait_send()


def by_kernel(wide, narrow, coef, velocity, slope_y):
    degrees = coef.shape[1]
    rows, gx_size = slope_y.shape[1:]
    kz_size, kx_size, gz_size = degrees * narrow, LANES * wide, rows * wide
    pairs = wide // 2
    values, slopes = z_tables(gz_size, kz_size)
    basis = x_table(gx_size, kx_size)
    zt = np.concatenate(
        [values.reshape(wide, rows, kz_size), slopes.reshape(wide, rows, kz_size)], axis=1
    )
    bt = np.ascontiguousarray(basis.T).reshape(pairs, 2 * LANES, gx_size)
    b = np.ascontiguousarray(basis.reshape(gx_size, pairs, 2 * LANES).transpose(1, 0, 2))
    vt = np.ascontiguousarray(values.T).reshape(narrow, degrees, gz_size)
    hbm = pl.BlockSpec(memory_space=pltpu.HBM)
    dma = pltpu.SemaphoreType.DMA
    return pl.pallas_call(
        functools.partial(kernel, wide, narrow, rows, gx_size),
        out_shape=(
            jax.ShapeDtypeStruct(coef.shape, BF16),
            jax.ShapeDtypeStruct(slope_y.shape, BF16),
        ),
        in_specs=[hbm] * 7,
        out_specs=(pl.BlockSpec(memory_space=pltpu.VMEM), hbm),
        scratch_shapes=[
            pltpu.VMEM(zt.shape, BF16),
            pltpu.VMEM(bt.shape, BF16),
            pltpu.VMEM(b.shape, BF16),
            pltpu.VMEM(vt.shape, BF16),
            pltpu.VMEM(velocity.shape, BF16),
            pltpu.VMEM(slope_y.shape, BF16),
            pltpu.VMEM((narrow, degrees, LANES), BF16),
            pltpu.VMEM((wide, 2 * rows, LANES), BF16),
            pltpu.VMEM((wide, 2 * rows, LANES), BF16),
            pltpu.VMEM((3 * rows, gx_size), F32),
            pltpu.VMEM((rows, gx_size), BF16),
            pltpu.VMEM(slope_y.shape, BF16),
            pltpu.VMEM((wide, rows, LANES), BF16),
            pltpu.VMEM((wide, rows, LANES), BF16),
            pltpu.VMEM((narrow, degrees, LANES), BF16),
            dma((8,)),
            dma((narrow,)),
            dma((narrow,)),
            dma((wide,)),
            dma((wide,)),
            dma((wide,)),
            dma((wide,)),
            dma((narrow,)),
            dma((narrow,)),
        ],
        compiler_params=pltpu.CompilerParams(
            collective_id=0, has_side_effects=True, vmem_limit_bytes=40 * 1024 * 1024
        ),
    )(coef, velocity, slope_y, zt, bt, b, vt)


def x_slope(wave_in, gx_size):
    width_now = wave_in.shape[-1]
    paired = wave_in.astype(F32).reshape(wave_in.shape[:-1] + (width_now // 2, 2))
    harmonic = lax.iota(jnp.int32, width_now // 2).astype(F32)
    omega_rate = harmonic * (2.0 * math.pi / gx_size)
    cos_part = omega_rate * paired[..., 1]
    sin_part = -omega_rate * paired[..., 0]
    return jnp.stack([cos_part, sin_part], axis=-1).reshape(wave_in.shape).astype(BF16)


def by_collectives(wide, narrow, coef, velocity, slope_y):
    gz_size, gx_size = slope_y.shape[1] * wide, slope_y.shape[2]
    kz_size, kx_size = coef.shape[1] * narrow, coef.shape[2] * wide
    values, slopes = z_tables(gz_size, kz_size)
    basis = x_table(gx_size, kx_size)
    einsum = functools.partial(jnp.einsum, preferred_element_type=F32)
    swap = functools.partial(lax.all_to_all, tiled=True)
    plane = swap(coef, "narrow", split_axis=0, concat_axis=1)
    wave_val = einsum("jn,ynk->yjk", values, plane).astype(BF16)
    wave_dz = einsum("jn,ynk->yjk", slopes, plane).astype(BF16)
    wave_val = swap(wave_val, "wide", split_axis=1, concat_axis=2)
    wave_dz = swap(wave_dz, "wide", split_axis=1, concat_axis=2)
    grid_val, grid_dx, grid_dz = (
        einsum("yjk,gk->yjg", field, basis)
        for field in (wave_val, x_slope(wave_val, gx_size), wave_dz)
    )
    total = velocity[0] * grid_dx + velocity[1] * slope_y.astype(F32) + velocity[2] * grid_dz
    half_coef = einsum("yjg,gk->yjk", (-total).astype(BF16), basis).astype(BF16)
    half_coef = swap(half_coef, "wide", split_axis=2, concat_axis=1)
    coef_z = einsum("jn,yjk->ynk", values, half_coef).astype(BF16)
    advect = swap(coef_z, "narrow", split_axis=1, concat_axis=0)
    return advect, grid_val.astype(BF16)


def solution(mesh):
    wide, narrow = mesh.shape["wide"], mesh.shape["narrow"]

    def on_device(coef, velocity, slope_y):
        whole_tiles = (
            slope_y.shape[0] == 1
            and coef.shape[1] % 16 == 0
            and coef.shape[2] == LANES
            and slope_y.shape[1] % 16 == 0
            and slope_y.shape[2] % 512 == 0
            and wide >= 4
            and wide & (wide - 1) == 0
        )
        plan = by_kernel if whole_tiles else by_collectives
        return plan(wide, narrow, coef, velocity, slope_y)

    return jax.shard_map(
        on_device,
        mesh=mesh,
        in_specs=(
            P(None, "narrow", "wide"),
            P(None, "narrow", "wide", None),
            P("narrow", "wide", None),
        ),
        out_specs=(P(None, "narrow", "wide"), P("narrow", "wide", None)),
        check_vma=False,
    )
```

profile of v0, /device:TPU:0, one launch (start us, length us, event | category | flops | bytes accessed | tf_op | source)
XLA Modules:
  0.0 41.8 jit_solution(15082350924804254090)
XLA Ops:
  0.6 0.0 copy-start
  0.6 1.9 %copy-done = bf16[4,1536,256]{2,1,0:T(8,128)(2,1)S(1)} copy-done((bf16[4,1536,256]{2,1,0:T(8,128)(2,1)S(1)}, bf16[4,1536,256]{2,1,0:T(8,128)(2,1)}, u32[]{:S(2)}) %copy-start) | copy-done | bytes 3145752
  2.5 0.0 copy-start.1
  2.5 1.9 %copy-done.1 = bf16[4,256,1536]{2,1,0:T(8,128)(2,1)S(1)} copy-done((bf16[4,256,1536]{2,1,0:T(8,128)(2,1)S(1)}, bf16[4,256,1536]{2,1,0:T(8,128)(2,1)}, u32[]{:S(2)}) %copy-start.1) | copy-done | bytes 3145752
  4.4 0.0 copy-start.2
  4.4 1.4 %copy-done.2 = bf16[8,192,512]{2,1,0:T(8,128)(2,1)S(1)} copy-done((bf16[8,192,512]{2,1,0:T(8,128)(2,1)S(1)}, bf16[8,192,512]{2,1,0:T(8,128)(2,1)}, u32[]{:S(2)}) %copy-start.2) | copy-done | bytes 1572888
  5.8 0.0 copy-start.3
  5.8 1.2 %copy-done.3 = bf16[3,1,96,1536]{3,2,1,0:T(8,128)(2,1)S(1)} copy-done((bf16[3,1,96,1536]{3,2,1,0:T(8,128)(2,1)S(1)}, bf16[3,1,96,1536]{3,2,1,0:T(8,128)(2,1)}, u32[]{:S(2)}) %copy-start.3) | copy-done | bytes 884760
  7.0 0.0 copy-start.4
  7.0 1.1 %copy-done.4 = bf16[4,128,768]{2,1,0:T(8,128)(2,1)S(1)} copy-done((bf16[4,128,768]{2,1,0:T(8,128)(2,1)S(1)}, bf16[4,128,768]{2,1,0:T(8,128)(2,1)}, u32[]{:S(2)}) %copy-start.4) | copy-done | bytes 786456
  8.1 0.0 copy-start.5
  8.1 1.0 %copy-done.5 = bf16[1,96,1536]{2,1,0:T(8,128)(2,1)S(1)} copy-done((bf16[1,96,1536]{2,1,0:T(8,128)(2,1)S(1)}, bf16[1,96,1536]{2,1,0:T(8,128)(2,1)}, u32[]{:S(2)}) %copy-start.5) | copy-done | bytes 294936
  9.1 0.0 copy-start.6
  9.1 0.9 %copy-done.6 = bf16[4,128,128]{2,1,0:T(8,128)(2,1)S(1)} copy-done((bf16[4,128,128]{2,1,0:T(8,128)(2,1)S(1)}, bf16[4,128,128]{2,1,0:T(8,128)(2,1)}, u32[]{:S(2)}) %copy-start.6) | copy-done | bytes 131096
  10.0 30.4 %shard_map.86 = (bf16[4,128,128]{2,1,0:T(8,128)(2,1)S(1)}, bf16[1,96,1536]{2,1,0:T(8,128)(2,1)S(1)}) custom-call(bf16[4,128,128]{2,1,0:T(8,128)(2,1)S(1)} %copy-done.6, bf16[3,1,96,1536]{3,2,1,0:T(8,128)(2,1)S(1)} %copy-done.3, bf16[1,96,1536]{2,1,0:T(8,128)(2,1)S(1)} %copy-done.5, bf16[8,192,512]{2,1,0:T(8,128)(2,1)S(1)} %copy-done.2, ...), custom_call_target="tpu_custom_call" | custom-call | tf_op jit(solution)/shard_map/pallas_call | solution.py:221
  40.4 0.7 %copy.11 = bf16[4,128,128]{2,1,0:T(8,128)(2,1)} copy(bf16[4,128,128]{2,1,0:T(8,128)(2,1)S(1)} %get-tuple-element.4) | data formatting | bytes 262144
  41.1 0.7 %copy.12 = bf16[1,96,1536]{2,1,0:T(8,128)(2,1)} copy(bf16[1,96,1536]{2,1,0:T(8,128)(2,1)S(1)} %get-tuple-element.5) | data formatting | bytes 589824
Async XLA Ops:
  0.6 1.9 %copy-start = (bf16[4,1536,256]{2,1,0:T(8,128)(2,1)S(1)}, bf16[4,1536,256]{2,1,0:T(8,128)(2,1)}, u32[]{:S(2)}) copy-start(bf16[4,1536,256]{2,1,0:T(8,128)(2,1)} %constant.10.clone.b_hbm) | copy-start | bytes 9437188
  2.5 1.9 %copy-start.1 = (bf16[4,256,1536]{2,1,0:T(8,128)(2,1)S(1)}, bf16[4,256,1536]{2,1,0:T(8,128)(2,1)}, u32[]{:S(2)}) copy-start(bf16[4,256,1536]{2,1,0:T(8,128)(2,1)} %constant.9.clone.bt_hbm) | copy-start | bytes 9437188
  4.4 1.4 %copy-start.2 = (bf16[8,192,512]{2,1,0:T(8,128)(2,1)S(1)}, bf16[8,192,512]{2,1,0:T(8,128)(2,1)}, u32[]{:S(2)}) copy-start(bf16[8,192,512]{2,1,0:T(8,128)(2,1)} %constant.8.clone.zt_hbm) | copy-start | bytes 4718596
  5.8 1.2 %copy-start.3 = (bf16[3,1,96,1536]{3,2,1,0:T(8,128)(2,1)S(1)}, bf16[3,1,96,1536]{3,2,1,0:T(8,128)(2,1)}, u32[]{:S(2)}) copy-start(bf16[3,1,96,1536]{3,2,1,0:T(8,128)(2,1)} %velocity.1) | copy-start | bytes 2654212
  7.0 1.1 %copy-start.4 = (bf16[4,128,768]{2,1,0:T(8,128)(2,1)S(1)}, bf16[4,128,768]{2,1,0:T(8,128)(2,1)}, u32[]{:S(2)}) copy-start(bf16[4,128,768]{2,1,0:T(8,128)(2,1)} %constant.11.clone.vt_hbm) | copy-start | bytes 2359300
  8.1 1.0 %copy-start.5 = (bf16[1,96,1536]{2,1,0:T(8,128)(2,1)S(1)}, bf16[1,96,1536]{2,1,0:T(8,128)(2,1)}, u32[]{:S(2)}) copy-start(bf16[1,96,1536]{2,1,0:T(8,128)(2,1)} %slope_y.1) | copy-start | bytes 884740
  9.1 0.9 %copy-start.6 = (bf16[4,128,128]{2,1,0:T(8,128)(2,1)S(1)}, bf16[4,128,128]{2,1,0:T(8,128)(2,1)}, u32[]{:S(2)}) copy-start(bf16[4,128,128]{2,1,0:T(8,128)(2,1)} %coef.1) | copy-start | bytes 393220
where the time goes:
time: 42.1 us; the launch traced here: 41.8 us
  Pallas kernels  30.4 us (72%)
  local copies, waits for them, and re-layouts  10.7 us (25%)
  between operations  0.65 us (2%)
    pallas_call x1, Pallas kernels, by_kernel(): pl.pallas_call(functools.partial(kernel, wide, narrow, rows, gx_size), ou...  30.4 us
    unnamed x16, local copies, waits for them, and re-layouts  10.7 us

commit v1 on v0

--- a/solution.py
+++ b/solution.py
@@ -14,6 +14,7 @@
 F32 = jnp.float32
 BF16 = jnp.bfloat16
 LANES = 128
+VMEM_BYTES = 64 * 1024 * 1024 - 256 * 1024
 
 
 def x_table(gx_size, kx_size):
@@ -195,12 +196,26 @@
     for peer in narrow_peers:
         send_f[peer] = dot(vt[peer], points).astype(BF16)
         push(send_f.at[peer], advect_out.at[m], f_send.at[peer], f_recv.at[m], {"narrow": peer})
-    advect_out[m] = dot(vt[m], points).astype(BF16)
+    send_f[m] = dot(vt[m], points).astype(BF16)
+    kept = pltpu.make_async_copy(send_f.at[m], advect_out.at[m], local_sem.at[8])
+    kept.start()
     for peer in narrow_peers:
         arrived(advect_out.at[peer], f_recv.at[peer], f_send.at[peer], {"narrow": peer})
+    kept.wait()
     grid_copy.wait()
     for copy in sends:
         copy.wait_send()
+
+
+def hand_over(advect, grid, advect_out, grid_out, sem):
+    copies = [
+        pltpu.make_async_copy(advect, advect_out, sem.at[0]),
+        pltpu.make_async_copy(grid, grid_out, sem.at[1]),
+    ]
+    for copy in copies:
+        copy.start()
+    for copy in copies:
+        copy.wait()
 
 
 def by_kernel(wide, narrow, coef, velocity, slope_y):
@@ -218,14 +233,14 @@
     vt = np.ascontiguousarray(values.T).reshape(narrow, degrees, gz_size)
     hbm = pl.BlockSpec(memory_space=pltpu.HBM)
     dma = pltpu.SemaphoreType.DMA
-    return pl.pallas_call(
+    advect, grid = pl.pallas_call(
         functools.partial(kernel, wide, narrow, rows, gx_size),
         out_shape=(
             jax.ShapeDtypeStruct(coef.shape, BF16),
             jax.ShapeDtypeStruct(slope_y.shape, BF16),
         ),
         in_specs=[hbm] * 7,
-        out_specs=(pl.BlockSpec(memory_space=pltpu.VMEM), hbm),
+        out_specs=(hbm, hbm),
         scratch_shapes=[
             pltpu.VMEM(zt.shape, BF16),
             pltpu.VMEM(bt.shape, BF16),
@@ -242,7 +257,7 @@
             pltpu.VMEM((wide, rows, LANES), BF16),
             pltpu.VMEM((wide, rows, LANES), BF16),
             pltpu.VMEM((narrow, degrees, LANES), BF16),
-            dma((8,)),
+            dma((9,)),
             dma((narrow,)),
             dma((narrow,)),
             dma((wide,)),
@@ -253,9 +268,20 @@
             dma((narrow,)),
         ],
         compiler_params=pltpu.CompilerParams(
-            collective_id=0, has_side_effects=True, vmem_limit_bytes=40 * 1024 * 1024
+            collective_id=0, has_side_effects=True, vmem_limit_bytes=VMEM_BYTES
         ),
     )(coef, velocity, slope_y, zt, bt, b, vt)
+    return pl.pallas_call(
+        hand_over,
+        out_shape=(
+            jax.ShapeDtypeStruct(coef.shape, BF16),
+            jax.ShapeDtypeStruct(slope_y.shape, BF16),
+        ),
+        in_specs=[hbm] * 2,
+        out_specs=(hbm, hbm),
+        scratch_shapes=[dma((2,))],
+        compiler_params=pltpu.CompilerParams(vmem_limit_bytes=VMEM_BYTES),
+    )(advect, grid)
 
 
 def x_slope(wave_in, gx_size):

time: 42.1 us -> 44.7 us (1.062)
  Pallas kernels: 30.4 us -> 43.9 us
  local copies, waits for them, and re-layouts: 10.7 us -> 0 us
    pallas_call x0 -> x1, Pallas kernels: none -> 14 us  [by_kernel(): pl.pallas_call(hand_over, out_shape=(jax.ShapeDtypeStruct(coef.shape, BF1...]
    unnamed x16 -> x0, local copies, waits for them, and re-layouts: 10.7 us -> none
    pallas_call x1, Pallas kernels: 30.4 us -> 29.9 us  [by_kernel(): pl.pallas_call(functools.partial(kernel, wide, narrow, rows, gx_size), ou...]
where the time goes in v1:
time: 44.7 us; the launch traced here: 44.5 us
  Pallas kernels  43.9 us (98%)
  between operations  0.64 us (1%)
    pallas_call x1, Pallas kernels, by_kernel(): pl.pallas_call(functools.partial(kernel, wide, narrow, rows, gx_size), ou...  29.9 us
    pallas_call x1, Pallas kernels, by_kernel(): pl.pallas_call(hand_over, out_shape=(jax.ShapeDtypeStruct(coef.shape, BF1...  14 us

profile of v1, /device:TPU:0, one launch (start us, length us, event | category | flops | bytes accessed | tf_op | source)
XLA Modules:
  0.0 44.5 jit_solution(34233174693296642)
XLA Ops:
  0.6 29.9 %shard_map.86 = (bf16[4,128,128]{2,1,0:T(8,128)(2,1)}, bf16[1,96,1536]{2,1,0:T(8,128)(2,1)}) custom-call(bf16[4,128,128]{2,1,0:T(8,128)(2,1)} %coef.1, bf16[3,1,96,1536]{3,2,1,0:T(8,128)(2,1)} %velocity.1, bf16[1,96,1536]{2,1,0:T(8,128)(2,1)} %slope_y.1, bf16[8,192,512]{2,1,0:T(8,128)(2,1)} %constant.8.clone.zt_hbm, ...), custom_call_target="tpu_custom_call" | custom-call | tf_op jit(solution)/shard_map/pallas_call | solution.py:236
  30.5 14.0 %shard_map.87 = (bf16[4,128,128]{2,1,0:T(8,128)(2,1)}, bf16[1,96,1536]{2,1,0:T(8,128)(2,1)}) custom-call(bf16[4,128,128]{2,1,0:T(8,128)(2,1)} %get-tuple-element.4.advect, bf16[1,96,1536]{2,1,0:T(8,128)(2,1)} %get-tuple-element.5.grid), custom_call_target="tpu_custom_call" | custom-call | tf_op jit(solution)/shard_map/pallas_call | solution.py:274

commit v2 on v1

--- a/solution.py
+++ b/solution.py
@@ -48,6 +48,10 @@
     return jnp.dot(left, right, preferred_element_type=F32)
 
 
+def dot_last(left, right):
+    return lax.dot_general(left, right, (((1,), (1,)), ((), ())), preferred_element_type=F32)
+
+
 def flip_bits(index, mask, size):
     total, bit = 0, 1
     while bit < size:
@@ -59,9 +63,9 @@
 
 def kernel(
     wide, narrow, rows, gx_size,
-    coef, velocity, slope_y, zt_hbm, bt_hbm, b_hbm, vt_hbm,
+    coef, velocity, slope_y, zt_hbm, bt_hbm, vt_hbm,
     advect_out, grid_out,
-    zt, bt, b, vt, speed, dy,
+    zt, bt, vt, speed, dy,
     recv_a, send_b, recv_b, acc, adv, buoy, send_e, recv_e, send_f,
     local_sem, a_send, a_recv, b_send, b_recv, e_send, e_recv, f_send, f_recv,
 ):
@@ -79,10 +83,10 @@
     loads = [
         pltpu.make_async_copy(src, dst, local_sem.at[1 + i])
         for i, (src, dst) in enumerate(
-            [(zt_hbm, zt), (bt_hbm, bt), (velocity, speed), (slope_y, dy), (b_hbm, b), (vt_hbm, vt)]
+            [(zt_hbm, zt), (bt_hbm, bt), (velocity, speed), (slope_y, dy), (vt_hbm, vt)]
         )
     ]
-    for load in loads:
+    for load in loads[:2]:
         load.start()
 
     barrier = pltpu.get_barrier_semaphore()
@@ -127,6 +131,8 @@
         send_points(2 * pair_of[t])
         send_points(2 * pair_of[t] + 1)
     send_points(beside)
+    for load in loads[2:]:
+        load.start()
     recv_b[w] = dot(zt[w], plane).astype(BF16)
 
     lane = lax.broadcasted_iota(jnp.int32, (1, LANES), 1)
@@ -175,19 +181,18 @@
                 total = total + speed[1, 0, :, cut].astype(F32) * dy[0, :, cut].astype(F32)
                 total = total + speed[2, 0, :, cut].astype(F32) * part[2 * rows :]
                 adv[:, cut] = (-total).astype(BF16)
-    grid_copy = pltpu.make_async_copy(buoy, grid_out, local_sem.at[7])
+    grid_copy = pltpu.make_async_copy(buoy, grid_out, local_sem.at[6])
     grid_copy.start()
 
-    loads[4].wait()
     for t in far_first + [0]:
         pair = pair_of[t]
-        half = dot(adv[...], b[pair]).astype(BF16)
+        half = dot_last(adv[...], bt[pair]).astype(BF16)
         for s in (0, 1):
             send_e[2 * pair + s] = half[:, s * LANES : (s + 1) * LANES]
         for d in (2 * pair, 2 * pair + 1) if t else (beside,):
             push(send_e.at[d], recv_e.at[w], e_send.at[d], e_recv.at[w], {"wide": d})
     recv_e[w] = send_e[w]
-    loads[5].wait()
+    loads[4].wait()
     for t in range(pairs):
         for d in (2 * pair_of[t], 2 * pair_of[t] + 1) if t else (beside,):
             arrived(recv_e.at[d], e_recv.at[d], e_send.at[d], {"wide": d})
@@ -197,7 +202,7 @@
         send_f[peer] = dot(vt[peer], points).astype(BF16)
         push(send_f.at[peer], advect_out.at[m], f_send.at[peer], f_recv.at[m], {"narrow": peer})
     send_f[m] = dot(vt[m], points).astype(BF16)
-    kept = pltpu.make_async_copy(send_f.at[m], advect_out.at[m], local_sem.at[8])
+    kept = pltpu.make_async_copy(send_f.at[m], advect_out.at[m], local_sem.at[7])
     kept.start()
     for peer in narrow_peers:
         arrived(advect_out.at[peer], f_recv.at[peer], f_send.at[peer], {"narrow": peer})
@@ -207,15 +212,21 @@
         copy.wait_send()
 
 
-def hand_over(advect, grid, advect_out, grid_out, sem):
-    copies = [
-        pltpu.make_async_copy(advect, advect_out, sem.at[0]),
-        pltpu.make_async_copy(grid, grid_out, sem.at[1]),
+def hand_over(advect, grid, advect_out, grid_out, advect_held, grid_held, sem):
+    routes = [(advect, advect_held, advect_out), (grid, grid_held, grid_out)]
+    fetches = [
+        pltpu.make_async_copy(src, held, sem.at[i]) for i, (src, held, _) in enumerate(routes)
     ]
-    for copy in copies:
-        copy.start()
-    for copy in copies:
-        copy.wait()
+    stores = [
+        pltpu.make_async_copy(held, dst, sem.at[2 + i]) for i, (_, held, dst) in enumerate(routes)
+    ]
+    for fetch in fetches:
+        fetch.start()
+    for fetch, store in zip(fetches, stores):
+        fetch.wait()
+        store.start()
+    for store in stores:
+        store.wait()
 
 
 def by_kernel(wide, narrow, coef, velocity, slope_y):
@@ -229,7 +240,6 @@
         [values.reshape(wide, rows, kz_size), slopes.reshape(wide, rows, kz_size)], axis=1
     )
     bt = np.ascontiguousarray(basis.T).reshape(pairs, 2 * LANES, gx_size)
-    b = np.ascontiguousarray(basis.reshape(gx_size, pairs, 2 * LANES).transpose(1, 0, 2))
     vt = np.ascontiguousarray(values.T).reshape(narrow, degrees, gz_size)
     hbm = pl.BlockSpec(memory_space=pltpu.HBM)
     dma = pltpu.SemaphoreType.DMA
@@ -239,12 +249,11 @@
             jax.ShapeDtypeStruct(coef.shape, BF16),
             jax.ShapeDtypeStruct(slope_y.shape, BF16),
         ),
-        in_specs=[hbm] * 7,
+        in_specs=[hbm] * 6,
         out_specs=(hbm, hbm),
         scratch_shapes=[
             pltpu.VMEM(zt.shape, BF16),
             pltpu.VMEM(bt.shape, BF16),
-            pltpu.VMEM(b.shape, BF16),
             pltpu.VMEM(vt.shape, BF16),
             pltpu.VMEM(velocity.shape, BF16),
             pltpu.VMEM(slope_y.shape, BF16),
@@ -257,7 +266,7 @@
             pltpu.VMEM((wide, rows, LANES), BF16),
             pltpu.VMEM((wide, rows, LANES), BF16),
             pltpu.VMEM((narrow, degrees, LANES), BF16),
-            dma((9,)),
+            dma((8,)),
             dma((narrow,)),
             dma((narrow,)),
             dma((wide,)),
@@ -270,7 +279,7 @@
         compiler_params=pltpu.CompilerParams(
             collective_id=0, has_side_effects=True, vmem_limit_bytes=VMEM_BYTES
         ),
-    )(coef, velocity, slope_y, zt, bt, b, vt)
+    )(coef, velocity, slope_y, zt, bt, vt)
     return pl.pallas_call(
         hand_over,
         out_shape=(
@@ -279,7 +288,11 @@
         ),
         in_specs=[hbm] * 2,
         out_specs=(hbm, hbm),
-        scratch_shapes=[dma((2,))],
+        scratch_shapes=[
+            pltpu.VMEM(coef.shape, BF16),
+            pltpu.VMEM(slope_y.shape, BF16),
+            dma((4,)),
+        ],
         compiler_params=pltpu.CompilerParams(vmem_limit_bytes=VMEM_BYTES),
     )(advect, grid)
 

time: 44.7 us -> 32.4 us (0.72)
  Pallas kernels: 43.9 us -> 31.6 us
    pallas_call x1, Pallas kernels: 14 us -> 1.78 us  [by_kernel(): pl.pallas_call(hand_over, out_shape=(jax.ShapeDtypeStruct(coef.shape, BF1...]
where the time goes in v2:
time: 32.4 us; the launch traced here: 32.2 us
  Pallas kernels  31.6 us (98%)
  between operations  0.64 us (2%)
    pallas_call x1, Pallas kernels, by_kernel(): pl.pallas_call(functools.partial(kernel, wide, narrow, rows, gx_size), ou...  29.8 us
    pallas_call x1, Pallas kernels, by_kernel(): pl.pallas_call(hand_over, out_shape=(jax.ShapeDtypeStruct(coef.shape, BF1...  1.78 us

profile of v2, /device:TPU:0, one launch (start us, length us, event | category | flops | bytes accessed | tf_op | source)
XLA Modules:
  0.0 32.2 jit_solution(7966274269777391555)
XLA Ops:
  0.6 29.8 %shard_map.77 = (bf16[4,128,128]{2,1,0:T(8,128)(2,1)}, bf16[1,96,1536]{2,1,0:T(8,128)(2,1)}) custom-call(bf16[4,128,128]{2,1,0:T(8,128)(2,1)} %coef.1, bf16[3,1,96,1536]{3,2,1,0:T(8,128)(2,1)} %velocity.1, bf16[1,96,1536]{2,1,0:T(8,128)(2,1)} %slope_y.1, bf16[8,192,512]{2,1,0:T(8,128)(2,1)} %constant.6.clone.zt_hbm, ...), custom_call_target="tpu_custom_call" | custom-call | tf_op jit(solution)/shard_map/pallas_call | solution.py:246
  30.4 1.8 %shard_map.78 = (bf16[4,128,128]{2,1,0:T(8,128)(2,1)}, bf16[1,96,1536]{2,1,0:T(8,128)(2,1)}) custom-call(bf16[4,128,128]{2,1,0:T(8,128)(2,1)} %get-tuple-element.4.advect, bf16[1,96,1536]{2,1,0:T(8,128)(2,1)} %get-tuple-element.5.grid), custom_call_target="tpu_custom_call" | custom-call | tf_op jit(solution)/shard_map/pallas_call | solution.py:283

commit v3 on v2

--- a/solution.py
+++ b/solution.py
@@ -62,7 +62,7 @@
 
 
 def kernel(
-    wide, narrow, rows, gx_size,
+    wide, narrow, groups, gx_size,
     coef, velocity, slope_y, zt_hbm, bt_hbm, vt_hbm,
     advect_out, grid_out,
     zt, bt, vt, speed, dy,
@@ -78,6 +78,9 @@
     pair_of = [flip_bits(mine, t, pairs) for t in range(pairs)]
     far_first = list(range(pairs - 1, 0, -1))
 
+    def others(t):
+        return (2 * pair_of[t], 2 * pair_of[t] + 1) if t else (beside,)
+
     own = pltpu.make_async_copy(coef.at[m], recv_a.at[m], local_sem.at[0])
     own.start()
     loads = [
@@ -123,17 +126,23 @@
 
     plane = recv_a[...].reshape(-1, LANES)
 
-    def send_points(d):
-        send_b[d] = dot(zt[d], plane).astype(BF16)
-        push(send_b.at[d], recv_b.at[w], b_send.at[d], b_recv.at[w], {"wide": d})
-
-    for t in far_first:
-        send_points(2 * pair_of[t])
-        send_points(2 * pair_of[t] + 1)
-    send_points(beside)
+    def of_group(g):
+        return pl.ds(2 * groups[g][0], 2 * groups[g][1])
+
+    def points_at(d, g):
+        return dot(zt[d, of_group(g)], plane).astype(BF16)
+
+    for g in range(len(groups)):
+        for t in far_first + [0]:
+            for d in others(t):
+                send_b[d, of_group(g)] = points_at(d, g)
+                push(
+                    send_b.at[d, of_group(g)], recv_b.at[w, of_group(g)],
+                    b_send.at[g, d], b_recv.at[g, w], {"wide": d},
+                )
+        recv_b[w, of_group(g)] = points_at(w, g)
     for load in loads[2:]:
         load.start()
-    recv_b[w] = dot(zt[w], plane).astype(BF16)
 
     lane = lax.broadcasted_iota(jnp.int32, (1, LANES), 1)
     even = lax.rem(lane, 2) == 0
@@ -146,56 +155,66 @@
         before = pltpu.roll(wide_field, 1, 1)
         return jnp.where(even, rate * after, -rate * before).astype(BF16)
 
-    def stacked(pair):
+    def stacked(pair, g):
+        count = groups[g][1]
         fields = []
         for s in (0, 1):
-            block = recv_b[2 * pair + s]
-            val, dz = block[:rows], block[rows:]
+            block = recv_b[2 * pair + s, of_group(g)]
+            val, dz = block[:count], block[count:]
             dx = slope_of(val, (2 * pair + s) * (LANES // 2))
             fields.append(jnp.concatenate([val, dx, dz], axis=0))
         return jnp.concatenate(fields, axis=1)
 
     tile = 512
     cuts = [slice(c, c + tile) for c in range(0, gx_size, tile)]
-    for t in range(pairs):
-        pair = pair_of[t]
-        if t == 0:
-            arrived(recv_b.at[beside], b_recv.at[beside], b_send.at[beside], {"wide": beside})
-            loads[1].wait()
-        else:
-            for d in (2 * pair, 2 * pair + 1):
-                arrived(recv_b.at[d], b_recv.at[d], b_send.at[d], {"wide": d})
-        fields = stacked(pair)
-        if t == pairs - 1:
-            loads[2].wait()
-            loads[3].wait()
-        for cut in cuts:
-            part = dot(fields, bt[pair, :, cut])
-            if t > 0:
-                part = part + acc[:, cut]
-            if t < pairs - 1:
-                acc[:, cut] = part
-            else:
-                buoy[0, :, cut] = part[:rows].astype(BF16)
-                total = speed[0, 0, :, cut].astype(F32) * part[rows : 2 * rows]
-                total = total + speed[1, 0, :, cut].astype(F32) * dy[0, :, cut].astype(F32)
-                total = total + speed[2, 0, :, cut].astype(F32) * part[2 * rows :]
-                adv[:, cut] = (-total).astype(BF16)
+    for g, (first, count) in enumerate(groups):
+        rows = slice(first, first + count)
+        for t in range(pairs):
+            pair = pair_of[t]
+            for d in others(t):
+                arrived(
+                    recv_b.at[d, of_group(g)], b_recv.at[g, d], b_send.at[g, d], {"wide": d}
+                )
+            fields = stacked(pair, g)
+            if g == 0 and t == 0:
+                loads[1].wait()
+            if g == 0 and t == pairs - 1:
+                loads[2].wait()
+                loads[3].wait()
+            for cut in cuts:
+                part = dot(fields, bt[pair, :, cut])
+                if t > 0:
+                    part = part + acc[: 3 * count, cut]
+                if t < pairs - 1:
+                    acc[: 3 * count, cut] = part
+                else:
+                    buoy[0, rows, cut] = part[:count].astype(BF16)
+                    total = speed[0, 0, rows, cut].astype(F32) * part[count : 2 * count]
+                    total = total + speed[1, 0, rows, cut].astype(F32) * dy[0, rows, cut].astype(F32)
+                    total = total + speed[2, 0, rows, cut].astype(F32) * part[2 * count :]
+                    adv[rows, cut] = (-total).astype(BF16)
+
+        for t in far_first + [0]:
+            pair = pair_of[t]
+            half = dot_last(adv[rows], bt[pair]).astype(BF16)
+            for s in (0, 1):
+                send_e[2 * pair + s, rows] = half[:, s * LANES : (s + 1) * LANES]
+            for d in others(t):
+                push(
+                    send_e.at[d, pl.ds(first, count)], recv_e.at[w, pl.ds(first, count)],
+                    e_send.at[g, d], e_recv.at[g, w], {"wide": d},
+                )
     grid_copy = pltpu.make_async_copy(buoy, grid_out, local_sem.at[6])
     grid_copy.start()
-
-    for t in far_first + [0]:
-        pair = pair_of[t]
-        half = dot_last(adv[...], bt[pair]).astype(BF16)
-        for s in (0, 1):
-            send_e[2 * pair + s] = half[:, s * LANES : (s + 1) * LANES]
-        for d in (2 * pair, 2 * pair + 1) if t else (beside,):
-            push(send_e.at[d], recv_e.at[w], e_send.at[d], e_recv.at[w], {"wide": d})
     recv_e[w] = send_e[w]
     loads[4].wait()
-    for t in range(pairs):
-        for d in (2 * pair_of[t], 2 * pair_of[t] + 1) if t else (beside,):
-            arrived(recv_e.at[d], e_recv.at[d], e_send.at[d], {"wide": d})
+    for g, (first, count) in enumerate(groups):
+        for t in range(pairs):
+            for d in others(t):
+                arrived(
+                    recv_e.at[d, pl.ds(first, count)], e_recv.at[g, d], e_send.at[g, d],
+                    {"wide": d},
+                )
 
     points = recv_e[...].reshape(-1, LANES)
     for peer in narrow_peers:
@@ -236,15 +255,24 @@
     pairs = wide // 2
     values, slopes = z_tables(gz_size, kz_size)
     basis = x_table(gx_size, kx_size)
+    early = max(16, rows * 2 // 3 // 16 * 16)
+    groups = [(0, early), (early, rows - early)] if early < rows else [(0, rows)]
+    values_at = values.reshape(wide, rows, kz_size)
+    slopes_at = slopes.reshape(wide, rows, kz_size)
     zt = np.concatenate(
-        [values.reshape(wide, rows, kz_size), slopes.reshape(wide, rows, kz_size)], axis=1
+        [
+            table[:, first : first + count]
+            for first, count in groups
+            for table in (values_at, slopes_at)
+        ],
+        axis=1,
     )
     bt = np.ascontiguousarray(basis.T).reshape(pairs, 2 * LANES, gx_size)
     vt = np.ascontiguousarray(values.T).reshape(narrow, degrees, gz_size)
     hbm = pl.BlockSpec(memory_space=pltpu.HBM)
     dma = pltpu.SemaphoreType.DMA
     advect, grid = pl.pallas_call(
-        functools.partial(kernel, wide, narrow, rows, gx_size),
+        functools.partial(kernel, wide, narrow, groups, gx_size),
         out_shape=(
             jax.ShapeDtypeStruct(coef.shape, BF16),
             jax.ShapeDtypeStruct(slope_y.shape, BF16),
@@ -260,7 +288,7 @@
             pltpu.VMEM((narrow, degrees, LANES), BF16),
             pltpu.VMEM((wide, 2 * rows, LANES), BF16),
             pltpu.VMEM((wide, 2 * rows, LANES), BF16),
-            pltpu.VMEM((3 * rows, gx_size), F32),
+            pltpu.VMEM((3 * groups[0][1], gx_size), F32),
             pltpu.VMEM((rows, gx_size), BF16),
             pltpu.VMEM(slope_y.shape, BF16),
             pltpu.VMEM((wide, rows, LANES), BF16),
@@ -269,10 +297,10 @@
             dma((8,)),
             dma((narrow,)),
             dma((narrow,)),
-            dma((wide,)),
-            dma((wide,)),
-            dma((wide,)),
-            dma((wide,)),
+            dma((len(groups), wide)),
+            dma((len(groups), wide)),
+            dma((len(groups), wide)),
+            dma((len(groups), wide)),
             dma((narrow,)),
             dma((narrow,)),
         ],

time: 32.4 us -> 34.2 us (1.056)
  Pallas kernels: 31.6 us -> 33.4 us
    pallas_call x1, Pallas kernels: 29.8 us -> 31.6 us  [by_kernel(): pl.pallas_call(functools.partial(kernel, wide, narrow, groups, gx_size),...]
where the time goes in v3:
time: 34.2 us; the launch traced here: 34 us
  Pallas kernels  33.4 us (98%)
  between operations  0.64 us (2%)
    pallas_call x1, Pallas kernels, by_kernel(): pl.pallas_call(functools.partial(kernel, wide, narrow, groups, gx_size),...  31.6 us
    pallas_call x1, Pallas kernels, by_kernel(): pl.pallas_call(hand_over, out_shape=(jax.ShapeDtypeStruct(coef.shape, BF1...  1.78 us

profile of v3, /device:TPU:0, one launch (start us, length us, event | category | flops | bytes accessed | tf_op | source)
XLA Modules:
  0.0 34.0 jit_solution(3790364864162325990)
XLA Ops:
  0.6 31.6 %shard_map.77 = (bf16[4,128,128]{2,1,0:T(8,128)(2,1)}, bf16[1,96,1536]{2,1,0:T(8,128)(2,1)}) custom-call(bf16[4,128,128]{2,1,0:T(8,128)(2,1)} %coef.1, bf16[3,1,96,1536]{3,2,1,0:T(8,128)(2,1)} %velocity.1, bf16[1,96,1536]{2,1,0:T(8,128)(2,1)} %slope_y.1, bf16[8,192,512]{2,1,0:T(8,128)(2,1)} %constant.6.clone.zt_hbm, ...), custom_call_target="tpu_custom_call" | custom-call | tf_op jit(solution)/shard_map/pallas_call | solution.py:274
  32.2 1.8 %shard_map.78 = (bf16[4,128,128]{2,1,0:T(8,128)(2,1)}, bf16[1,96,1536]{2,1,0:T(8,128)(2,1)}) custom-call(bf16[4,128,128]{2,1,0:T(8,128)(2,1)} %get-tuple-element.4.advect, bf16[1,96,1536]{2,1,0:T(8,128)(2,1)} %get-tuple-element.5.grid), custom_call_target="tpu_custom_call" | custom-call | tf_op jit(solution)/shard_map/pallas_call | solution.py:311

commit v4 on v2

--- a/solution.py
+++ b/solution.py
@@ -63,10 +63,10 @@
 
 def kernel(
     wide, narrow, rows, gx_size,
-    coef, velocity, slope_y, zt_hbm, bt_hbm, vt_hbm,
+    coef, velocity, slope_y, order, order_back, zt_hbm, bt_hbm, vt_hbm,
     advect_out, grid_out,
     zt, bt, vt, speed, dy,
-    recv_a, send_b, recv_b, acc, adv, buoy, send_e, recv_e, send_f,
+    recv_a, send_b, recv_b, acc, adv, buoy, send_e, recv_e, points, send_f,
     local_sem, a_send, a_recv, b_send, b_recv, e_send, e_recv, f_send, f_recv,
 ):
     pairs = wide // 2
@@ -121,7 +121,7 @@
     for peer in narrow_peers:
         arrived(recv_a.at[peer], a_recv.at[peer], a_send.at[peer], {"narrow": peer})
 
-    plane = recv_a[...].reshape(-1, LANES)
+    plane = dot(recv_a[...].reshape(-1, LANES), order[...]).astype(BF16)
 
     def send_points(d):
         send_b[d] = dot(zt[d], plane).astype(BF16)
@@ -138,70 +138,91 @@
     lane = lax.broadcasted_iota(jnp.int32, (1, LANES), 1)
     even = lax.rem(lane, 2) == 0
 
+    low = lane < LANES // 2
+    local = 2 * lax.div(lax.rem(lane, LANES // 2), 2) + lax.div(lane, LANES // 2)
+
     def slope_of(field, first):
-        harmonic = (lax.div(lane, 2) + first).astype(F32)
-        rate = harmonic * (2.0 * math.pi / gx_size)
-        wide_field = field.astype(F32)
-        after = pltpu.roll(wide_field, LANES - 1, 1)
-        before = pltpu.roll(wide_field, 1, 1)
-        return jnp.where(even, rate * after, -rate * before).astype(BF16)
+        rate = (local + first).astype(F32) * (2.0 * math.pi / gx_size)
+        after = pltpu.roll(field, LANES - 1, 1)
+        before = pltpu.roll(field, 1, 1)
+        return jnp.where(even, rate * after, -rate * before)
 
     def stacked(pair):
         fields = []
         for s in (0, 1):
-            block = recv_b[2 * pair + s]
+            block = recv_b[2 * pair + s].astype(F32)
             val, dz = block[:rows], block[rows:]
             dx = slope_of(val, (2 * pair + s) * (LANES // 2))
             fields.append(jnp.concatenate([val, dx, dz], axis=0))
-        return jnp.concatenate(fields, axis=1)
-
-    tile = 512
-    cuts = [slice(c, c + tile) for c in range(0, gx_size, tile)]
-    for t in range(pairs):
-        pair = pair_of[t]
-        if t == 0:
-            arrived(recv_b.at[beside], b_recv.at[beside], b_send.at[beside], {"wide": beside})
+        return split(*fields)
+
+    def split(first, second):
+        turned = [pltpu.roll(field, LANES // 2, 1) for field in (first, second)]
+        return (
+            jnp.where(low, first, turned[1]).astype(BF16),
+            jnp.where(low, turned[0], second).astype(BF16),
+        )
+
+    quads = pairs // 2
+    quad_of = [lax.div(pair_of[2 * u], 2) for u in range(quads)]
+    middle = gx_size // 2
+    tile = 256
+    cuts = [slice(c, c + tile) for c in range(0, middle, tile)]
+    for u in range(quads):
+        quad = quad_of[u]
+        for t in (2 * u, 2 * u + 1):
+            for d in (2 * pair_of[t], 2 * pair_of[t] + 1) if t else (beside,):
+                arrived(recv_b.at[d], b_recv.at[d], b_send.at[d], {"wide": d})
+        both = [stacked(2 * quad), stacked(2 * quad + 1)]
+        fields = [jnp.concatenate([half[i] for half in both], axis=1) for i in (0, 1)]
+        if u == 0:
             loads[1].wait()
-        else:
-            for d in (2 * pair, 2 * pair + 1):
-                arrived(recv_b.at[d], b_recv.at[d], b_send.at[d], {"wide": d})
-        fields = stacked(pair)
-        if t == pairs - 1:
+        if u == quads - 1:
             loads[2].wait()
             loads[3].wait()
         for cut in cuts:
-            part = dot(fields, bt[pair, :, cut])
-            if t > 0:
-                part = part + acc[:, cut]
-            if t < pairs - 1:
-                acc[:, cut] = part
+            parts = [dot(fields[i], bt[quad, i, :, cut]) for i in (0, 1)]
+            if u > 0:
+                parts = [parts[i] + acc[i, :, cut] for i in (0, 1)]
+            if u < quads - 1:
+                for i in (0, 1):
+                    acc[i, :, cut] = parts[i]
             else:
-                buoy[0, :, cut] = part[:rows].astype(BF16)
-                total = speed[0, 0, :, cut].astype(F32) * part[rows : 2 * rows]
-                total = total + speed[1, 0, :, cut].astype(F32) * dy[0, :, cut].astype(F32)
-                total = total + speed[2, 0, :, cut].astype(F32) * part[2 * rows :]
-                adv[:, cut] = (-total).astype(BF16)
+                totals = []
+                for part, start in ((parts[0] + parts[1], 0), (parts[0] - parts[1], middle)):
+                    at = slice(cut.start + start, cut.stop + start)
+                    buoy[0, :, at] = part[:rows].astype(BF16)
+                    total = speed[0, 0, :, at].astype(F32) * part[rows : 2 * rows]
+                    total = total + speed[1, 0, :, at].astype(F32) * dy[0, :, at].astype(F32)
+                    totals.append(total + speed[2, 0, :, at].astype(F32) * part[2 * rows :])
+                adv[0, :, cut] = (-(totals[0] + totals[1])).astype(BF16)
+                adv[1, :, cut] = (totals[1] - totals[0]).astype(BF16)
     grid_copy = pltpu.make_async_copy(buoy, grid_out, local_sem.at[6])
     grid_copy.start()
 
-    for t in far_first + [0]:
-        pair = pair_of[t]
-        half = dot_last(adv[...], bt[pair]).astype(BF16)
+    for u in reversed(range(quads)):
+        quad = quad_of[u]
+        halves = [dot_last(adv[i], bt[quad, i]) for i in (0, 1)]
         for s in (0, 1):
-            send_e[2 * pair + s] = half[:, s * LANES : (s + 1) * LANES]
-        for d in (2 * pair, 2 * pair + 1) if t else (beside,):
-            push(send_e.at[d], recv_e.at[w], e_send.at[d], e_recv.at[w], {"wide": d})
-    recv_e[w] = send_e[w]
+            columns = slice(s * LANES, (s + 1) * LANES)
+            first, second = split(halves[0][:, columns], halves[1][:, columns])
+            send_e[4 * quad + 2 * s] = first
+            send_e[4 * quad + 2 * s + 1] = second
+        for t in (2 * u + 1, 2 * u):
+            for d in (2 * pair_of[t], 2 * pair_of[t] + 1) if t else (beside,):
+                push(send_e.at[d], recv_e.at[w], e_send.at[d], e_recv.at[w], {"wide": d})
+    points[w] = dot(send_e[w], order_back[...]).astype(BF16)
     loads[4].wait()
     for t in range(pairs):
         for d in (2 * pair_of[t], 2 * pair_of[t] + 1) if t else (beside,):
             arrived(recv_e.at[d], e_recv.at[d], e_send.at[d], {"wide": d})
-
-    points = recv_e[...].reshape(-1, LANES)
-    for peer in narrow_peers:
-        send_f[peer] = dot(vt[peer], points).astype(BF16)
+            points[d] = dot(recv_e[d], order_back[...]).astype(BF16)
+
+    all_points = points[...].reshape(-1, LANES)
+    for peer in narrow_peers:
+        send_f[peer] = dot(vt[peer], all_points).astype(BF16)
         push(send_f.at[peer], advect_out.at[m], f_send.at[peer], f_recv.at[m], {"narrow": peer})
-    send_f[m] = dot(vt[m], points).astype(BF16)
+    send_f[m] = dot(vt[m], all_points).astype(BF16)
     kept = pltpu.make_async_copy(send_f.at[m], advect_out.at[m], local_sem.at[7])
     kept.start()
     for peer in narrow_peers:
@@ -239,7 +260,14 @@
     zt = np.concatenate(
         [values.reshape(wide, rows, kz_size), slopes.reshape(wide, rows, kz_size)], axis=1
     )
-    bt = np.ascontiguousarray(basis.T).reshape(pairs, 2 * LANES, gx_size)
+    order_of = np.arange(LANES).reshape(-1, 2, 2).transpose(1, 0, 2).reshape(-1)
+    order = np.zeros((LANES, LANES), ml_dtypes.bfloat16)
+    order[order_of, np.arange(LANES)] = 1
+    order_back = np.ascontiguousarray(order.T)
+    bt = np.ascontiguousarray(
+        basis[: gx_size // 2].T.reshape(pairs // 2, 4 * LANES // 4, 2, 2, gx_size // 2)
+        .transpose(0, 2, 1, 3, 4).reshape(pairs // 2, 2, 2 * LANES, gx_size // 2)
+    )
     vt = np.ascontiguousarray(values.T).reshape(narrow, degrees, gz_size)
     hbm = pl.BlockSpec(memory_space=pltpu.HBM)
     dma = pltpu.SemaphoreType.DMA
@@ -249,7 +277,7 @@
             jax.ShapeDtypeStruct(coef.shape, BF16),
             jax.ShapeDtypeStruct(slope_y.shape, BF16),
         ),
-        in_specs=[hbm] * 6,
+        in_specs=[hbm] * 3 + [pl.BlockSpec(memory_space=pltpu.VMEM)] * 2 + [hbm] * 3,
         out_specs=(hbm, hbm),
         scratch_shapes=[
             pltpu.VMEM(zt.shape, BF16),
@@ -260,9 +288,10 @@
             pltpu.VMEM((narrow, degrees, LANES), BF16),
             pltpu.VMEM((wide, 2 * rows, LANES), BF16),
             pltpu.VMEM((wide, 2 * rows, LANES), BF16),
-            pltpu.VMEM((3 * rows, gx_size), F32),
-            pltpu.VMEM((rows, gx_size), BF16),
+            pltpu.VMEM((2, 3 * rows, gx_size // 2), F32),
+            pltpu.VMEM((2, rows, gx_size // 2), BF16),
             pltpu.VMEM(slope_y.shape, BF16),
+            pltpu.VMEM((wide, rows, LANES), BF16),
             pltpu.VMEM((wide, rows, LANES), BF16),
             pltpu.VMEM((wide, rows, LANES), BF16),
             pltpu.VMEM((narrow, degrees, LANES), BF16),
@@ -279,7 +308,7 @@
         compiler_params=pltpu.CompilerParams(
             collective_id=0, has_side_effects=True, vmem_limit_bytes=VMEM_BYTES
         ),
-    )(coef, velocity, slope_y, zt, bt, vt)
+    )(coef, velocity, slope_y, order, order_back, zt, bt, vt)
     return pl.pallas_call(
         hand_over,
         out_shape=(

time: 32.4 us -> 33.3 us (1.028)
  Pallas kernels: 31.6 us -> 32.4 us
    pallas_call x1, Pallas kernels: 29.8 us -> 30.7 us  [by_kernel(): pl.pallas_call(functools.partial(kernel, wide, narrow, rows, gx_size), ou...]
where the time goes in v4:
time: 33.3 us; the launch traced here: 33.1 us
  Pallas kernels  32.4 us (97%)
  between operations  0.64 us (2%)
    pallas_call x1, Pallas kernels, by_kernel(): pl.pallas_call(functools.partial(kernel, wide, narrow, rows, gx_size), ou...  30.7 us
    pallas_call x1, Pallas kernels, by_kernel(): pl.pallas_call(hand_over, out_shape=(jax.ShapeDtypeStruct(coef.shape, BF1...  1.78 us

profile of v4, /device:TPU:0, one launch (start us, length us, event | category | flops | bytes accessed | tf_op | source)
XLA Modules:
  0.0 33.1 jit_solution(10406990495568986768)
XLA Ops:
  0.6 30.7 %shard_map.95 = (bf16[4,128,128]{2,1,0:T(8,128)(2,1)}, bf16[1,96,1536]{2,1,0:T(8,128)(2,1)}) custom-call(bf16[4,128,128]{2,1,0:T(8,128)(2,1)} %coef.1, bf16[3,1,96,1536]{3,2,1,0:T(8,128)(2,1)} %velocity.1, bf16[1,96,1536]{2,1,0:T(8,128)(2,1)} %slope_y.1, bf16[128,128]{1,0:T(8,128)(2,1)} %constant.10.clone.order, bf16[128,128]{1,0:T(8,128)(2,1)} %constant.11.clone.order_back, ...), custom_call_target="tpu_custom_call" | custom-call | tf_op jit(solution)/shard_map/pallas_call | solution.py:274
  31.3 1.8 %shard_map.96 = (bf16[4,128,128]{2,1,0:T(8,128)(2,1)}, bf16[1,96,1536]{2,1,0:T(8,128)(2,1)}) custom-call(bf16[4,128,128]{2,1,0:T(8,128)(2,1)} %get-tuple-element.4.advect, bf16[1,96,1536]{2,1,0:T(8,128)(2,1)} %get-tuple-element.5.grid), custom_call_target="tpu_custom_call" | custom-call | tf_op jit(solution)/shard_map/pallas_call | solution.py:312

commit v5 on v3

--- a/solution.py
+++ b/solution.py
@@ -132,14 +132,18 @@
     def points_at(d, g):
         return dot(zt[d, of_group(g)], plane).astype(BF16)
 
+    def send_points(g, d):
+        push(
+            send_b.at[d, of_group(g)], recv_b.at[w, of_group(g)],
+            b_send.at[g, d], b_recv.at[g, w], {"wide": d},
+        )
+
     for g in range(len(groups)):
         for t in far_first + [0]:
             for d in others(t):
                 send_b[d, of_group(g)] = points_at(d, g)
-                push(
-                    send_b.at[d, of_group(g)], recv_b.at[w, of_group(g)],
-                    b_send.at[g, d], b_recv.at[g, w], {"wide": d},
-                )
+                if g == 0:
+                    send_points(g, d)
         recv_b[w, of_group(g)] = points_at(w, g)
     for load in loads[2:]:
         load.start()
@@ -171,6 +175,12 @@
         rows = slice(first, first + count)
         for t in range(pairs):
             pair = pair_of[t]
+            if g == 0 and t == pairs // 2:
+                while sends:
+                    sends.pop(0).wait_send()
+                for later in range(1, len(groups)):
+                    for peer in [d for u in far_first + [0] for d in others(u)]:
+                        send_points(later, peer)
             for d in others(t):
                 arrived(
                     recv_b.at[d, of_group(g)], b_recv.at[g, d], b_send.at[g, d], {"wide": d}

time: 34.2 us -> 33.6 us (0.982)
  Pallas kernels: 33.4 us -> 32.8 us
    pallas_call x1, Pallas kernels: 31.6 us -> 31 us  [by_kernel(): pl.pallas_call(functools.partial(kernel, wide, narrow, groups, gx_size),...]
where the time goes in v5:
time: 33.6 us; the launch traced here: 33.4 us
  Pallas kernels  32.8 us (98%)
  between operations  0.64 us (2%)
    pallas_call x1, Pallas kernels, by_kernel(): pl.pallas_call(functools.partial(kernel, wide, narrow, groups, gx_size),...  31 us
    pallas_call x1, Pallas kernels, by_kernel(): pl.pallas_call(hand_over, out_shape=(jax.ShapeDtypeStruct(coef.shape, BF1...  1.78 us

profile of v5, /device:TPU:0, one launch (start us, length us, event | category | flops | bytes accessed | tf_op | source)
XLA Modules:
  0.0 33.4 jit_solution(16260696181920199428)
XLA Ops:
  0.6 31.0 %shard_map.77 = (bf16[4,128,128]{2,1,0:T(8,128)(2,1)}, bf16[1,96,1536]{2,1,0:T(8,128)(2,1)}) custom-call(bf16[4,128,128]{2,1,0:T(8,128)(2,1)} %coef.1, bf16[3,1,96,1536]{3,2,1,0:T(8,128)(2,1)} %velocity.1, bf16[1,96,1536]{2,1,0:T(8,128)(2,1)} %slope_y.1, bf16[8,192,512]{2,1,0:T(8,128)(2,1)} %constant.6.clone.zt_hbm, ...), custom_call_target="tpu_custom_call" | custom-call | tf_op jit(solution)/shard_map/pallas_call | solution.py:284
  31.6 1.8 %shard_map.78 = (bf16[4,128,128]{2,1,0:T(8,128)(2,1)}, bf16[1,96,1536]{2,1,0:T(8,128)(2,1)}) custom-call(bf16[4,128,128]{2,1,0:T(8,128)(2,1)} %get-tuple-element.4.advect, bf16[1,96,1536]{2,1,0:T(8,128)(2,1)} %get-tuple-element.5.grid), custom_call_target="tpu_custom_call" | custom-call | tf_op jit(solution)/shard_map/pallas_call | solution.py:321

commit v6 on v2

--- a/solution.py
+++ b/solution.py
@@ -14,7 +14,7 @@
 F32 = jnp.float32
 BF16 = jnp.bfloat16
 LANES = 128
-VMEM_BYTES = 64 * 1024 * 1024 - 256 * 1024
+VMEM_BYTES = 64 * 1024 * 1024 - 640 * 1024
 
 
 def x_table(gx_size, kx_size):
@@ -212,23 +212,6 @@
         copy.wait_send()
 
 
-def hand_over(advect, grid, advect_out, grid_out, advect_held, grid_held, sem):
-    routes = [(advect, advect_held, advect_out), (grid, grid_held, grid_out)]
-    fetches = [
-        pltpu.make_async_copy(src, held, sem.at[i]) for i, (src, held, _) in enumerate(routes)
-    ]
-    stores = [
-        pltpu.make_async_copy(held, dst, sem.at[2 + i]) for i, (_, held, dst) in enumerate(routes)
-    ]
-    for fetch in fetches:
-        fetch.start()
-    for fetch, store in zip(fetches, stores):
-        fetch.wait()
-        store.start()
-    for store in stores:
-        store.wait()
-
-
 def by_kernel(wide, narrow, coef, velocity, slope_y):
     degrees = coef.shape[1]
     rows, gx_size = slope_y.shape[1:]
@@ -243,7 +226,7 @@
     vt = np.ascontiguousarray(values.T).reshape(narrow, degrees, gz_size)
     hbm = pl.BlockSpec(memory_space=pltpu.HBM)
     dma = pltpu.SemaphoreType.DMA
-    advect, grid = pl.pallas_call(
+    return pl.pallas_call(
         functools.partial(kernel, wide, narrow, rows, gx_size),
         out_shape=(
             jax.ShapeDtypeStruct(coef.shape, BF16),
@@ -280,21 +263,6 @@
             collective_id=0, has_side_effects=True, vmem_limit_bytes=VMEM_BYTES
         ),
     )(coef, velocity, slope_y, zt, bt, vt)
-    return pl.pallas_call(
-        hand_over,
-        out_shape=(
-            jax.ShapeDtypeStruct(coef.shape, BF16),
-            jax.ShapeDtypeStruct(slope_y.shape, BF16),
-        ),
-        in_specs=[hbm] * 2,
-        out_specs=(hbm, hbm),
-        scratch_shapes=[
-            pltpu.VMEM(coef.shape, BF16),
-            pltpu.VMEM(slope_y.shape, BF16),
-            dma((4,)),
-        ],
-        compiler_params=pltpu.CompilerParams(vmem_limit_bytes=VMEM_BYTES),
-    )(advect, grid)
 
 
 def x_slope(wave_in, gx_size):

time: 32.4 us -> 33.9 us (1.046)
  local copies, waits for them, and re-layouts: 0 us -> 3.26 us
  Pallas kernels: 31.6 us -> 29.8 us
    unnamed x0 -> x2, local copies, waits for them, and re-layouts: none -> 3.26 us
    pallas_call x1 -> x0, Pallas kernels: 1.78 us -> none  [by_kernel(): pl.pallas_call(hand_over, out_shape=(jax.ShapeDtypeStruct(coef.shape, BF1...]
where the time goes in v6:
time: 33.9 us; the launch traced here: 33.7 us
  Pallas kernels  29.8 us (88%)
  local copies, waits for them, and re-layouts  3.26 us (10%)
  between operations  0.64 us (2%)
    pallas_call x1, Pallas kernels, by_kernel(): pl.pallas_call(functools.partial(kernel, wide, narrow, rows, gx_size), ou...  29.8 us
    unnamed x2, local copies, waits for them, and re-layouts  3.26 us

profile of v6, /device:TPU:0, one launch (start us, length us, event | category | flops | bytes accessed | tf_op | source)
XLA Modules:
  0.0 33.7 jit_solution(17047587688513635219)
XLA Ops:
  0.6 29.8 %shard_map.77 = (bf16[4,128,128]{2,1,0:T(8,128)(2,1)}, bf16[1,96,1536]{2,1,0:T(8,128)(2,1)}) custom-call(bf16[4,128,128]{2,1,0:T(8,128)(2,1)} %coef.1, bf16[3,1,96,1536]{3,2,1,0:T(8,128)(2,1)} %velocity.1, bf16[1,96,1536]{2,1,0:T(8,128)(2,1)} %slope_y.1, bf16[8,192,512]{2,1,0:T(8,128)(2,1)} %constant.6.clone.zt_hbm, ...), custom_call_target="tpu_custom_call" | custom-call | tf_op jit(solution)/shard_map/pallas_call | solution.py:229
  30.4 1.6 %copy.10 = bf16[4,128,128]{2,1,0:T(8,128)(2,1)} copy(bf16[4,128,128]{2,1,0:T(8,128)(2,1)} %get-tuple-element.4) | data formatting | bytes 262144
  32.0 1.7 %copy.11 = bf16[1,96,1536]{2,1,0:T(8,128)(2,1)} copy(bf16[1,96,1536]{2,1,0:T(8,128)(2,1)} %get-tuple-element.5) | data formatting | bytes 589824

commit v7 on v2

--- a/solution.py
+++ b/solution.py
@@ -123,14 +123,13 @@
 
     plane = recv_a[...].reshape(-1, LANES)
 
-    def send_points(d):
-        send_b[d] = dot(zt[d], plane).astype(BF16)
-        push(send_b.at[d], recv_b.at[w], b_send.at[d], b_recv.at[w], {"wide": d})
-
-    for t in far_first:
-        send_points(2 * pair_of[t])
-        send_points(2 * pair_of[t] + 1)
-    send_points(beside)
+    for t in far_first + [0]:
+        both = pl.ds(2 * pair_of[t], 2)
+        fields = dot(zt[both].reshape(4 * rows, -1), plane).astype(BF16)
+        send_b[both] = fields.reshape(2, 2 * rows, LANES)
+        for d in (2 * pair_of[t], 2 * pair_of[t] + 1) if t else (beside,):
+            push(send_b.at[d], recv_b.at[w], b_send.at[d], b_recv.at[w], {"wide": d})
+    recv_b[w] = send_b[w]
     for load in loads[2:]:
         load.start()
     recv_b[w] = dot(zt[w], plane).astype(BF16)

time: 32.4 us -> 32.5 us (level)
  no operation moved by 1% of the time
where the time goes in v7:
time: 32.5 us; the launch traced here: 32.4 us
  Pallas kernels  31.7 us (98%)
  between operations  0.64 us (2%)
    pallas_call x1, Pallas kernels, by_kernel(): pl.pallas_call(functools.partial(kernel, wide, narrow, rows, gx_size), ou...  29.9 us
    pallas_call x1, Pallas kernels, by_kernel(): pl.pallas_call(hand_over, out_shape=(jax.ShapeDtypeStruct(coef.shape, BF1...  1.78 us

profile of v7, /device:TPU:0, one launch (start us, length us, event | category | flops | bytes accessed | tf_op | source)
XLA Modules:
  0.0 32.4 jit_solution(3749237802778227016)
XLA Ops:
  0.6 29.9 %shard_map.77 = (bf16[4,128,128]{2,1,0:T(8,128)(2,1)}, bf16[1,96,1536]{2,1,0:T(8,128)(2,1)}) custom-call(bf16[4,128,128]{2,1,0:T(8,128)(2,1)} %coef.1, bf16[3,1,96,1536]{3,2,1,0:T(8,128)(2,1)} %velocity.1, bf16[1,96,1536]{2,1,0:T(8,128)(2,1)} %slope_y.1, bf16[8,192,512]{2,1,0:T(8,128)(2,1)} %constant.6.clone.zt_hbm, ...), custom_call_target="tpu_custom_call" | custom-call | tf_op jit(solution)/shard_map/pallas_call | solution.py:245
  30.6 1.8 %shard_map.78 = (bf16[4,128,128]{2,1,0:T(8,128)(2,1)}, bf16[1,96,1536]{2,1,0:T(8,128)(2,1)}) custom-call(bf16[4,128,128]{2,1,0:T(8,128)(2,1)} %get-tuple-element.4.advect, bf16[1,96,1536]{2,1,0:T(8,128)(2,1)} %get-tuple-element.5.grid), custom_call_target="tpu_custom_call" | custom-call | tf_op jit(solution)/shard_map/pallas_call | solution.py:282
